TPU v7x, 512 devices: a whole 4x4x16 slice. The times are simulated.
512 devices in a mesh: dp: 32 (over z, core), crow: 4 (over x), ccol: 4 (over y).
Axes of the slice: x: 4, y: 4, z: 16, core: 2. Of those that a mesh axis runs over, the one named last changes fastest.
Arguments:
- data: float32 [16, 262144], P(None, ('dp', 'crow')), may hold values from 0 to 1
- centres: float32 [16, 3072], P(None, 'ccol'), may hold values from 0 to 1
- scales: float32 [16], replicated, may hold values from 0.5 to 1.2
- factor: float32 [3072, 3072], P('crow', 'ccol'), may hold values from -1 to 1, as said below
- block_inv: float32 [12, 256, 256], P('crow'), may hold values from -1 to 2
- iterate: float32 [8, 3072], replicated, may hold values from -6 to 6
- residual: float32 [8, 3072], replicated, may hold values from -6 to 6
- direction: float32 [8, 3072], replicated, may hold values from -6 to 6
Outputs:
- new_iterate: float32 [8, 3072], replicated
- new_residual: float32 [8, 3072], replicated
- new_direction: float32 [8, 3072], replicated
Inputs may be any that keep to these rules, and one draw needn't show every extreme that they name: `factor`: blocks of 256 x 256 on and above the block diagonal are zero.
All inputs are finite; a program needn't handle non-finite values.
Results may differ from a plain program's by a relative error of at most 0.0001.
Values sent between devices are 32-bit elements; how exact they have to be, the bound alone decides.
A program may use at most 64 MiB of HBM per device.

v0:
```python
import jax
import jax.numpy as jnp
from jax import lax
from jax.sharding import PartitionSpec as P

RBLK = 1024
ridge_weight = 0.2
highest = lax.Precision.HIGHEST


def kernel_tile(sample, centre_set, scales):
    scaled_sample = sample / scales[:, None]
    scaled_centres = centre_set / scales[:, None]
    cross_terms = lax.dot_general(
        scaled_centres,
        scaled_sample,
        (((0,), (0,)), ((), ())),
        precision=highest,
        preferred_element_type=jnp.float32,
    )
    distance = (
        jnp.sum(scaled_centres * scaled_centres, axis=0)[:, None]
        + jnp.sum(scaled_sample * scaled_sample, axis=0)[None, :]
        - 2.0 * cross_terms
    )
    return jnp.exp(-0.5 * distance)


def project(weights, tile):
    return jnp.dot(weights, tile, precision=highest, preferred_element_type=jnp.float32)


def pullback(images, tile):
    return lax.dot_general(
        images,
        tile,
        (((1,), (1,)), ((), ())),
        precision=highest,
        preferred_element_type=jnp.float32,
    )


def per_device(data, centres, scales, factor, block_inv, iterate, residual, direction):
    order = block_inv.shape[1]
    local_rows = factor.shape[0]
    local_cols = factor.shape[1]
    per_row = local_rows // order
    per_col = local_cols // order
    nblocks = per_row * lax.axis_size("crow")
    row_place = lax.axis_index("crow")
    col_place = lax.axis_index("ccol")
    solved = jnp.zeros_like(direction)
    for number in reversed(range(nblocks)):
        start = number * order
        owner = number // per_col
        offset = number % per_col * order
        held = number % per_row
        segment = lax.dynamic_slice_in_dim(solved, row_place * local_rows, local_rows, 1)
        partial_value = project(segment, factor[:, offset : offset + order])
        partial_value = jnp.where(col_place == owner, partial_value, 0.0)
        partial_value = lax.psum(partial_value, ("crow", "ccol"))
        piece = project(direction[:, start : start + order] - partial_value, block_inv[held])
        solved = solved.at[:, start : start + order].set(piece)
    own_part = lax.dynamic_slice_in_dim(solved, row_place * local_rows, local_rows, 1)
    solved = lax.all_gather(own_part, "crow", axis=1, tiled=True)
    rows_here = data.shape[1]
    span = min(RBLK, rows_here)
    blocks = rows_here // span
    stacked = data.reshape(data.shape[0], blocks, span).transpose(1, 0, 2)
    width = centres.shape[1]
    mine = lax.dynamic_slice_in_dim(solved, col_place * width, width, 1)

    def forward_images(carry, sample):
        return (carry, project(mine, kernel_tile(sample, centres, scales)))

    _, images = lax.scan(forward_images, jnp.zeros((), jnp.float32), stacked)
    images = lax.psum(images, "ccol")

    def backward_images(total, pair):
        sample, image_rows = pair
        return (total + pullback(image_rows, kernel_tile(sample, centres, scales)), None)

    summed, _ = lax.scan(
        backward_images, jnp.zeros((solved.shape[0], width), jnp.float32), (stacked, images)
    )
    summed = lax.psum(summed, ("dp", "crow"))
    summed = lax.all_gather(summed, "ccol", axis=1, tiled=True)
    total_rows = rows_here * lax.axis_size("dp") * lax.axis_size("crow")
    normal_image = summed / total_rows + ridge_weight * solved
    image = jnp.zeros_like(direction)
    for number in range(nblocks):
        start = number * order
        owner = number // per_row
        held = number % per_row
        offset = held * order
        segment = lax.dynamic_slice_in_dim(image, col_place * local_cols, local_cols, 1)
        leading = jnp.where(col_place == 0, normal_image[:, start : start + order], 0.0)
        term = pullback(
            leading - pullback(segment, factor[offset : offset + order, :]), block_inv[held]
        )
        term = jnp.where(row_place == owner, term, 0.0)
        piece = lax.psum(term, ("crow", "ccol"))
        image = image.at[:, start : start + order].set(piece)
    gamma = jnp.sum(residual * residual, axis=1)
    curvature = jnp.sum(direction * image, axis=1)
    alpha = (gamma / curvature)[:, None]
    new_iterate = iterate + alpha * direction
    new_residual = residual - alpha * image
    gamma_next = jnp.sum(new_residual * new_residual, axis=1)
    new_direction = new_residual + (gamma_next / gamma)[:, None] * direction
    return (new_iterate, new_residual, new_direction)


def solution(mesh):
    placed = (
        P(None, ("dp", "crow")),
        P(None, "ccol"),
        P(),
        P("crow", "ccol"),
        P("crow", None, None),
        P(),
        P(),
        P(),
    )
    return jax.shard_map(
        per_device, mesh=mesh, in_specs=placed, out_specs=(P(), P(), P()), check_vma=False
    )
```

profile of v0, /device:TPU:8, one launch (start us, length us, event | category | flops | bytes accessed | tf_op | source)
XLA Modules:
  0.0 1564.1 jit_solution(2935731484131593567)
XLA Ops:
  16.1 41.8 %psum.182 = f32[8,256]{1,0:T(8,128)S(1)} all-reduce(f32[8,256]{1,0:T(8,128)S(1)} %convolution_select_fusion.34), channel_id=1, replica_groups=mesh['dp'=32,'crow'=4,'ccol'=4] {'crow','ccol'}, use_global_device_ids=true, to_apply=%region_2.3 | all-reduce | flops 2048 | bytes 16384 | tf_op jit(solution)/shard_map/psum | solution.py:61
  60.6 36.0 %psum.183 = f32[8,256]{1,0:T(8,128)S(1)} all-reduce(f32[8,256]{1,0:T(8,128)S(1)} %convolution_select_fusion.33), channel_id=1, replica_groups=mesh['dp'=32,'crow'=4,'ccol'=4] {'crow','ccol'}, use_global_device_ids=true, to_apply=%region_4.5 | all-reduce | flops 2048 | bytes 16384 | tf_op jit(solution)/shard_map/psum | solution.py:61
  98.9 38.1 %psum.184 = f32[8,256]{1,0:T(8,128)S(1)} all-reduce(f32[8,256]{1,0:T(8,128)S(1)} %convolution_select_fusion.31), channel_id=1, replica_groups=mesh['dp'=32,'crow'=4,'ccol'=4] {'crow','ccol'}, use_global_device_ids=true, to_apply=%region_6.7 | all-reduce | flops 2048 | bytes 16384 | tf_op jit(solution)/shard_map/psum | solution.py:61
  138.8 35.9 %psum.185 = f32[8,256]{1,0:T(8,128)S(1)} all-reduce(f32[8,256]{1,0:T(8,128)S(1)} %convolution_select_fusion.29), channel_id=1, replica_groups=mesh['dp'=32,'crow'=4,'ccol'=4] {'crow','ccol'}, use_global_device_ids=true, to_apply=%region_8.9 | all-reduce | flops 2048 | bytes 16384 | tf_op jit(solution)/shard_map/psum | solution.py:61
  176.1 38.2 %psum.186 = f32[8,256]{1,0:T(8,128)S(1)} all-reduce(f32[8,256]{1,0:T(8,128)S(1)} %convolution_select_fusion.27), channel_id=1, replica_groups=mesh['dp'=32,'crow'=4,'ccol'=4] {'crow','ccol'}, use_global_device_ids=true, to_apply=%region_10.11 | all-reduce | flops 2048 | bytes 16384 | tf_op jit(solution)/shard_map/psum | solution.py:61
  215.6 36.0 %psum.187 = f32[8,256]{1,0:T(8,128)S(1)} all-reduce(f32[8,256]{1,0:T(8,128)S(1)} %convolution_select_fusion.25), channel_id=1, replica_groups=mesh['dp'=32,'crow'=4,'ccol'=4] {'crow','ccol'}, use_global_device_ids=true, to_apply=%region_12.13 | all-reduce | flops 2048 | bytes 16384 | tf_op jit(solution)/shard_map/psum | solution.py:61
  252.7 38.0 %psum.188 = f32[8,256]{1,0:T(8,128)S(1)} all-reduce(f32[8,256]{1,0:T(8,128)S(1)} %convolution_select_fusion.23), channel_id=1, replica_groups=mesh['dp'=32,'crow'=4,'ccol'=4] {'crow','ccol'}, use_global_device_ids=true, to_apply=%region_14.15 | all-reduce | flops 2048 | bytes 16384 | tf_op jit(solution)/shard_map/psum | solution.py:61
  291.9 36.0 %psum.189 = f32[8,256]{1,0:T(8,128)S(1)} all-reduce(f32[8,256]{1,0:T(8,128)S(1)} %convolution_select_fusion.21), channel_id=1, replica_groups=mesh['dp'=32,'crow'=4,'ccol'=4] {'crow','ccol'}, use_global_device_ids=true, to_apply=%region_16.17 | all-reduce | flops 2048 | bytes 16384 | tf_op jit(solution)/shard_map/psum | solution.py:61
  329.2 38.0 %psum.190 = f32[8,256]{1,0:T(8,128)S(1)} all-reduce(f32[8,256]{1,0:T(8,128)S(1)} %convolution_select_fusion.19), channel_id=1, replica_groups=mesh['dp'=32,'crow'=4,'ccol'=4] {'crow','ccol'}, use_global_device_ids=true, to_apply=%region_18.19 | all-reduce | flops 2048 | bytes 16384 | tf_op jit(solution)/shard_map/psum | solution.py:61
  368.4 36.0 %psum.191 = f32[8,256]{1,0:T(8,128)S(1)} all-reduce(f32[8,256]{1,0:T(8,128)S(1)} %convolution_select_fusion.17), channel_id=1, replica_groups=mesh['dp'=32,'crow'=4,'ccol'=4] {'crow','ccol'}, use_global_device_ids=true, to_apply=%region_20.21 | all-reduce | flops 2048 | bytes 16384 | tf_op jit(solution)/shard_map/psum | solution.py:61
  405.6 38.0 %psum.192 = f32[8,256]{1,0:T(8,128)S(1)} all-reduce(f32[8,256]{1,0:T(8,128)S(1)} %convolution_select_fusion.15), channel_id=1, replica_groups=mesh['dp'=32,'crow'=4,'ccol'=4] {'crow','ccol'}, use_global_device_ids=true, to_apply=%region_22.23 | all-reduce | flops 2048 | bytes 16384 | tf_op jit(solution)/shard_map/psum | solution.py:61
  444.9 36.0 %psum.193 = f32[8,256]{1,0:T(8,128)S(1)} all-reduce(f32[8,256]{1,0:T(8,128)S(1)} %convolution_select_fusion.13), channel_id=1, replica_groups=mesh['dp'=32,'crow'=4,'ccol'=4] {'crow','ccol'}, use_global_device_ids=true, to_apply=%region_23.24 | all-reduce | flops 2048 | bytes 16384 | tf_op jit(solution)/shard_map/psum | solution.py:61
  481.7 12.1 all_gather.6
  495.6 12.0 while.45
  508.7 55.2 %all-reduce.4.cloned.1.call-done = f32[2,8,1024]{2,1,0:T(8,128)} async-done(((f32[2,8,1024]{2,1,0:T(8,128)}), f32[2,8,1024]{2,1,0:T(8,128)}) %all-reduce.4.cloned.1.call-update) | async-done | bytes 65552 | tf_op jit(solution)/shard_map/psum | solution.py:77
  563.9 20.4 %while.46 = (s32[]{:T(128)}, f32[8,768]{1,0:T(8,128)}, f32[2,8,1024]{2,1,0:T(8,128)}, f32[16]{0:T(128)S(1)}, f32[16,768]{1,0:T(8,128)S(1)}, /*index=5*/f32[2,16,1024]{2,1,0:T(8,128)S(1)}, s32[]{:T(128)}, s32[]{:T(128)}) while((s32[]{:T(128)}, f32[8,768]{1,0:T(8,128)}, f32[2,8,1024]{2,1,0:T(8,128)}, f32[16]{0:T(128)S(1)}, ...), condition=%wide.region_32.33_spmd.clone, body=%wide.region_29.32_spmd.clone.sunk | while | flops 229763328 | bytes 6618855 | solution.py:83
  568.5 5.6 fusion.224
  578.6 5.6 fusion.224
  584.3 494.7 %psum.195 = f32[8,768]{1,0:T(8,128)S(1)} all-reduce(f32[8,768]{1,0:T(8,128)} %get-tuple-element.356), channel_id=1, replica_groups=mesh['dp'=32,'crow'=4,'ccol'=4] {'dp','crow'}, use_global_device_ids=true, to_apply=%region_33.34 | all-reduce | flops 6144 | bytes 49152 | tf_op jit(solution)/shard_map/psum | solution.py:86
  1079.0 11.8 all_gather.7
  1091.8 37.8 %psum.196 = f32[8,256]{1,0:T(8,128)S(1)} all-reduce(f32[8,256]{1,0:T(8,128)S(1)} %convolution_select_fusion.11), channel_id=1, replica_groups=mesh['dp'=32,'crow'=4,'ccol'=4] {'crow','ccol'}, use_global_device_ids=true, to_apply=%region_34.35 | all-reduce | flops 2048 | bytes 16384 | tf_op jit(solution)/shard_map/psum | solution.py:102
  1131.2 36.5 %psum.197 = f32[8,256]{1,0:T(8,128)S(1)} all-reduce(f32[8,256]{1,0:T(8,128)S(1)} %convolution_select_fusion.10), channel_id=1, replica_groups=mesh['dp'=32,'crow'=4,'ccol'=4] {'crow','ccol'}, use_global_device_ids=true, to_apply=%region_35.36 | all-reduce | flops 2048 | bytes 16384 | tf_op jit(solution)/shard_map/psum | solution.py:102
  1169.3 37.6 %psum.198 = f32[8,256]{1,0:T(8,128)S(1)} all-reduce(f32[8,256]{1,0:T(8,128)S(1)} %convolution_select_fusion.9), channel_id=1, replica_groups=mesh['dp'=32,'crow'=4,'ccol'=4] {'crow','ccol'}, use_global_device_ids=true, to_apply=%region_36.37 | all-reduce | flops 2048 | bytes 16384 | tf_op jit(solution)/shard_map/psum | solution.py:102
  1208.4 36.6 %psum.199 = f32[8,256]{1,0:T(8,128)S(1)} all-reduce(f32[8,256]{1,0:T(8,128)S(1)} %convolution_select_fusion.8), channel_id=1, replica_groups=mesh['dp'=32,'crow'=4,'ccol'=4] {'crow','ccol'}, use_global_device_ids=true, to_apply=%region_37.38 | all-reduce | flops 2048 | bytes 16384 | tf_op jit(solution)/shard_map/psum | solution.py:102
  1246.7 37.5 %psum.200 = f32[8,256]{1,0:T(8,128)S(1)} all-reduce(f32[8,256]{1,0:T(8,128)S(1)} %convolution_select_fusion.7), channel_id=1, replica_groups=mesh['dp'=32,'crow'=4,'ccol'=4] {'crow','ccol'}, use_global_device_ids=true, to_apply=%region_38.39 | all-reduce | flops 2048 | bytes 16384 | tf_op jit(solution)/shard_map/psum | solution.py:102
  1285.8 36.5 %psum.201 = f32[8,256]{1,0:T(8,128)S(1)} all-reduce(f32[8,256]{1,0:T(8,128)S(1)} %convolution_select_fusion.6), channel_id=1, replica_groups=mesh['dp'=32,'crow'=4,'ccol'=4] {'crow','ccol'}, use_global_device_ids=true, to_apply=%region_39.40 | all-reduce | flops 2048 | bytes 16384 | tf_op jit(solution)/shard_map/psum | solution.py:102
  1324.0 37.5 %psum.202 = f32[8,256]{1,0:T(8,128)S(1)} all-reduce(f32[8,256]{1,0:T(8,128)S(1)} %convolution_select_fusion.5), channel_id=1, replica_groups=mesh['dp'=32,'crow'=4,'ccol'=4] {'crow','ccol'}, use_global_device_ids=true, to_apply=%region_40.41 | all-reduce | flops 2048 | bytes 16384 | tf_op jit(solution)/shard_map/psum | solution.py:102
  1363.1 36.5 %psum.203 = f32[8,256]{1,0:T(8,128)S(1)} all-reduce(f32[8,256]{1,0:T(8,128)S(1)} %convolution_select_fusion.4), channel_id=1, replica_groups=mesh['dp'=32,'crow'=4,'ccol'=4] {'crow','ccol'}, use_global_device_ids=true, to_apply=%region_41.42 | all-reduce | flops 2048 | bytes 16384 | tf_op jit(solution)/shard_map/psum | solution.py:102
  1401.3 37.6 %psum.204 = f32[8,256]{1,0:T(8,128)S(1)} all-reduce(f32[8,256]{1,0:T(8,128)S(1)} %convolution_select_fusion.3), channel_id=1, replica_groups=mesh['dp'=32,'crow'=4,'ccol'=4] {'crow','ccol'}, use_global_device_ids=true, to_apply=%region_42.43 | all-reduce | flops 2048 | bytes 16384 | tf_op jit(solution)/shard_map/psum | solution.py:102
  1440.5 36.5 %psum.205 = f32[8,256]{1,0:T(8,128)S(1)} all-reduce(f32[8,256]{1,0:T(8,128)S(1)} %convolution_select_fusion.2), channel_id=1, replica_groups=mesh['dp'=32,'crow'=4,'ccol'=4] {'crow','ccol'}, use_global_device_ids=true, to_apply=%region_43.44 | all-reduce | flops 2048 | bytes 16384 | tf_op jit(solution)/shard_map/psum | solution.py:102
  1478.6 37.5 %psum.206 = f32[8,256]{1,0:T(8,128)S(1)} all-reduce(f32[8,256]{1,0:T(8,128)S(1)} %convolution_select_fusion.1), channel_id=1, replica_groups=mesh['dp'=32,'crow'=4,'ccol'=4] {'crow','ccol'}, use_global_device_ids=true, to_apply=%region_44.45 | all-reduce | flops 2048 | bytes 16384 | tf_op jit(solution)/shard_map/psum | solution.py:102
  1517.8 36.5 %psum.207 = f32[8,256]{1,0:T(8,128)S(1)} all-reduce(f32[8,256]{1,0:T(8,128)S(1)} %convolution_select_fusion), channel_id=1, replica_groups=mesh['dp'=32,'crow'=4,'ccol'=4] {'crow','ccol'}, use_global_device_ids=true, to_apply=%region_45.46 | all-reduce | flops 2048 | bytes 16384 | tf_op jit(solution)/shard_map/psum | solution.py:102
  (116 shorter events, 72.2 us)
Async XLA Ops:
  7.2 91.3 %copy-start = (f32[768,768]{1,0:T(8,128)S(1)}, f32[768,768]{1,0:T(8,128)}, u32[]{:S(2)}) copy-start(f32[768,768]{1,0:T(8,128)} %param.63) | copy-start | bytes 7077892
  7.2 129.8 %copy-start.1 = (f32[3,256,256]{2,1,0:T(8,128)S(1)}, f32[3,256,256]{2,1,0:T(8,128)}, u32[]{:S(2)}) copy-start(f32[3,256,256]{2,1,0:T(8,128)} %param.64) | copy-start | bytes 2359300
  7.2 167.6 %copy-start.3 = (f32[8,3072]{1,0:T(8,128)S(1)}, f32[8,3072]{1,0:T(8,128)}, u32[]{:S(2)}) copy-start(f32[8,3072]{1,0:T(8,128)} %param.67) | copy-start | bytes 294916
  7.2 556.7 %all-reduce.4.cloned.1.call-start = ((), (), s32[]{:S(2)}) async-start(), calls=%async_computation | async-start | bytes 131072 | tf_op jit(solution)/shard_map/psum | solution.py:77
  328.7 165.1 %copy-start.6 = (f32[16,2048]{1,0:T(8,128)S(1)}, f32[16,2048]{1,0:T(8,128)}, u32[]{:S(2)}) copy-start(f32[16,2048]{1,0:T(8,128)} %param.60) | copy-start | bytes 393220
  329.2 166.4 %copy-start.2 = (f32[16,768]{1,0:T(8,128)S(1)}, f32[16,768]{1,0:T(8,128)}, u32[]{:S(2)}) copy-start(f32[16,768]{1,0:T(8,128)} %param.61) | copy-start | bytes 147460
  329.2 166.4 %copy-start.4 = (f32[16]{0:T(128)S(1)}, f32[16]{0:T(128)}, u32[]{:S(2)}) copy-start(f32[16]{0:T(128)} %param.62) | copy-start | bytes 196
  1555.5 1.7 copy-start.5
Sparse Core Ops, SparseCore 0:
  507.7 56.0 all-reduce.3
where the time goes:
time: 1570 us; the launch traced here: 1560 us
  blocking collectives  1410 us (90%)
  matrix products  62.8 us (4%)
  waiting for transfers between devices  55.2 us (4%)
  other arithmetic  18.8 us (1%)
    psum x1, blocking collectives, per_device(): summed = lax.psum(summed, ('dp', 'crow'))  495 us
    psum x12, blocking collectives, per_device(): partial_value = lax.psum(partial_value, ('crow', 'ccol'))  448 us
    psum x12, blocking collectives, per_device(): piece = lax.psum(term, ('crow', 'ccol'))  445 us
    psum x1, waiting for transfers between devices, per_device(): images = lax.psum(images, 'ccol')  55.2 us
  transfers between devices with their start and end apart: 1, of which 1 were waited for; matrix products, arithmetic and copies ran while one was open for 0% of the time, Pallas kernels for 0%

commit v1 on v0

--- a/solution.py
+++ b/solution.py
@@ -83,7 +83,7 @@
     summed, _ = lax.scan(
         backward_images, jnp.zeros((solved.shape[0], width), jnp.float32), (stacked, images)
     )
-    summed = lax.psum(summed, ("dp", "crow"))
+    summed = jnp.sum(lax.all_gather(summed, ("dp", "crow")), axis=0)
     summed = lax.all_gather(summed, "ccol", axis=1, tiled=True)
     total_rows = rows_here * lax.axis_size("dp") * lax.axis_size("crow")
     normal_image = summed / total_rows + ridge_weight * solved

time: 1570 us -> 1220 us (0.78)
  blocking collectives: 1410 us -> 918 us
  waiting for transfers between devices: 55.2 us -> 198 us
    psum x1 -> x0, blocking collectives: 495 us -> none  [per_device(): summed = lax.psum(summed, ('dp', 'crow'))]
    all_gather x0 -> x1, waiting for transfers between devices: none -> 141 us  [per_device(): summed = jnp.sum(lax.all_gather(summed, ('dp', 'crow')), axis=0)]
  transfers between devices with their start and end apart: 1 -> 2, of which waited for: 1 -> 2; matrix products, arithmetic and copies ran while one was open for 0% -> 0% of each run, Pallas kernels for 0% -> 0%
where the time goes in v1:
time: 1220 us
  blocking collectives  918 us (75%)
  waiting for transfers between devices  198 us (16%)
  matrix products  62.8 us (5%)
  other arithmetic  21.6 us (2%)
  between operations  14.5 us (1%)
    psum x12, blocking collectives, per_device(): partial_value = lax.psum(partial_value, ('crow', 'ccol'))  448 us
    psum x12, blocking collectives, per_device(): piece = lax.psum(term, ('crow', 'ccol'))  447 us
    all_gather x1, waiting for transfers between devices, per_device(): summed = jnp.sum(lax.all_gather(summed, ('dp', 'crow')), axis=0)  141 us
    psum x1, waiting for transfers between devices, per_device(): images = lax.psum(images, 'ccol')  56.2 us
    dot_general x26, matrix products, project(): jnp.dot(weights, tile, precision=highest, preferred_element_type=jnp.floa...  25.3 us
  transfers between devices with their start and end apart: 2, of which 2 were waited for; matrix products, arithmetic and copies ran while one was open for 0% of the time, Pallas kernels for 0%

profile of v1, /device:TPU:8, one launch (start us, length us, event | category | flops | bytes accessed | tf_op | source)
XLA Modules:
  0.0 1216.8 jit_solution(15168731489971087196)
XLA Ops:
  16.1 41.8 %psum.175 = f32[8,256]{1,0:T(8,128)S(1)} all-reduce(f32[8,256]{1,0:T(8,128)S(1)} %convolution_select_fusion.34), channel_id=1, replica_groups=mesh['dp'=32,'crow'=4,'ccol'=4] {'crow','ccol'}, use_global_device_ids=true, to_apply=%region_2.3 | all-reduce | flops 2048 | bytes 16384 | tf_op jit(solution)/shard_map/psum | solution.py:61
  60.6 36.0 %psum.176 = f32[8,256]{1,0:T(8,128)S(1)} all-reduce(f32[8,256]{1,0:T(8,128)S(1)} %convolution_select_fusion.33), channel_id=1, replica_groups=mesh['dp'=32,'crow'=4,'ccol'=4] {'crow','ccol'}, use_global_device_ids=true, to_apply=%region_4.5 | all-reduce | flops 2048 | bytes 16384 | tf_op jit(solution)/shard_map/psum | solution.py:61
  98.9 38.1 %psum.177 = f32[8,256]{1,0:T(8,128)S(1)} all-reduce(f32[8,256]{1,0:T(8,128)S(1)} %convolution_select_fusion.31), channel_id=1, replica_groups=mesh['dp'=32,'crow'=4,'ccol'=4] {'crow','ccol'}, use_global_device_ids=true, to_apply=%region_6.7 | all-reduce | flops 2048 | bytes 16384 | tf_op jit(solution)/shard_map/psum | solution.py:61
  138.8 35.9 %psum.178 = f32[8,256]{1,0:T(8,128)S(1)} all-reduce(f32[8,256]{1,0:T(8,128)S(1)} %convolution_select_fusion.29), channel_id=1, replica_groups=mesh['dp'=32,'crow'=4,'ccol'=4] {'crow','ccol'}, use_global_device_ids=true, to_apply=%region_8.9 | all-reduce | flops 2048 | bytes 16384 | tf_op jit(solution)/shard_map/psum | solution.py:61
  176.1 38.2 %psum.179 = f32[8,256]{1,0:T(8,128)S(1)} all-reduce(f32[8,256]{1,0:T(8,128)S(1)} %convolution_select_fusion.27), channel_id=1, replica_groups=mesh['dp'=32,'crow'=4,'ccol'=4] {'crow','ccol'}, use_global_device_ids=true, to_apply=%region_10.11 | all-reduce | flops 2048 | bytes 16384 | tf_op jit(solution)/shard_map/psum | solution.py:61
  215.5 36.0 %psum.180 = f32[8,256]{1,0:T(8,128)S(1)} all-reduce(f32[8,256]{1,0:T(8,128)S(1)} %convolution_select_fusion.25), channel_id=1, replica_groups=mesh['dp'=32,'crow'=4,'ccol'=4] {'crow','ccol'}, use_global_device_ids=true, to_apply=%region_12.13 | all-reduce | flops 2048 | bytes 16384 | tf_op jit(solution)/shard_map/psum | solution.py:61
  252.7 38.0 %psum.181 = f32[8,256]{1,0:T(8,128)S(1)} all-reduce(f32[8,256]{1,0:T(8,128)S(1)} %convolution_select_fusion.23), channel_id=1, replica_groups=mesh['dp'=32,'crow'=4,'ccol'=4] {'crow','ccol'}, use_global_device_ids=true, to_apply=%region_14.15 | all-reduce | flops 2048 | bytes 16384 | tf_op jit(solution)/shard_map/psum | solution.py:61
  291.9 36.0 %psum.182 = f32[8,256]{1,0:T(8,128)S(1)} all-reduce(f32[8,256]{1,0:T(8,128)S(1)} %convolution_select_fusion.21), channel_id=1, replica_groups=mesh['dp'=32,'crow'=4,'ccol'=4] {'crow','ccol'}, use_global_device_ids=true, to_apply=%region_16.17 | all-reduce | flops 2048 | bytes 16384 | tf_op jit(solution)/shard_map/psum | solution.py:61
  329.2 38.0 %psum.183 = f32[8,256]{1,0:T(8,128)S(1)} all-reduce(f32[8,256]{1,0:T(8,128)S(1)} %convolution_select_fusion.19), channel_id=1, replica_groups=mesh['dp'=32,'crow'=4,'ccol'=4] {'crow','ccol'}, use_global_device_ids=true, to_apply=%region_18.19 | all-reduce | flops 2048 | bytes 16384 | tf_op jit(solution)/shard_map/psum | solution.py:61
  368.4 36.0 %psum.184 = f32[8,256]{1,0:T(8,128)S(1)} all-reduce(f32[8,256]{1,0:T(8,128)S(1)} %convolution_select_fusion.17), channel_id=1, replica_groups=mesh['dp'=32,'crow'=4,'ccol'=4] {'crow','ccol'}, use_global_device_ids=true, to_apply=%region_20.21 | all-reduce | flops 2048 | bytes 16384 | tf_op jit(solution)/shard_map/psum | solution.py:61
  405.6 38.0 %psum.185 = f32[8,256]{1,0:T(8,128)S(1)} all-reduce(f32[8,256]{1,0:T(8,128)S(1)} %convolution_select_fusion.15), channel_id=1, replica_groups=mesh['dp'=32,'crow'=4,'ccol'=4] {'crow','ccol'}, use_global_device_ids=true, to_apply=%region_22.23 | all-reduce | flops 2048 | bytes 16384 | tf_op jit(solution)/shard_map/psum | solution.py:61
  444.9 36.0 %psum.186 = f32[8,256]{1,0:T(8,128)S(1)} all-reduce(f32[8,256]{1,0:T(8,128)S(1)} %convolution_select_fusion.13), channel_id=1, replica_groups=mesh['dp'=32,'crow'=4,'ccol'=4] {'crow','ccol'}, use_global_device_ids=true, to_apply=%region_23.24 | all-reduce | flops 2048 | bytes 16384 | tf_op jit(solution)/shard_map/psum | solution.py:61
  481.7 12.1 all_gather.12
  495.6 12.0 while.45
  507.7 56.2 %all-reduce.4.cloned.1.call-done = f32[2,8,1024]{2,1,0:T(8,128)} async-done(((f32[2,8,1024]{2,1,0:T(8,128)}), f32[2,8,1024]{2,1,0:T(8,128)}) %all-reduce.4.cloned.1.call-update) | async-done | bytes 65552 | tf_op jit(solution)/shard_map/psum | solution.py:77
  563.9 20.4 %while.46 = (s32[]{:T(128)}, f32[8,768]{1,0:T(8,128)}, f32[2,8,1024]{2,1,0:T(8,128)}, f32[16]{0:T(128)S(1)}, f32[16,768]{1,0:T(8,128)S(1)}, /*index=5*/f32[2,16,1024]{2,1,0:T(8,128)S(1)}, s32[]{:T(128)}, s32[]{:T(128)}) while((s32[]{:T(128)}, f32[8,768]{1,0:T(8,128)}, f32[2,8,1024]{2,1,0:T(8,128)}, f32[16]{0:T(128)S(1)}, ...), condition=%wide.region_32.33_spmd.clone, body=%wide.region_29.32_spmd.clone.sunk | while | flops 229763328 | bytes 6618855 | solution.py:83
  568.5 5.6 fusion.224
  578.7 5.6 fusion.224
  585.8 141.4 %all-gather.3.cloned.1.call-done = f32[1024,768]{1,0:T(8,128)} async-done(((f32[8,768]{1,0:T(8,128)}), f32[1024,768]{1,0:T(8,128)}) %all-gather.3.cloned.1.call-update) | async-done | bytes 3145744 | tf_op jit(solution)/shard_map/all_gather | solution.py:86
  729.3 12.1 all_gather.15
  742.4 36.7 %psum.188 = f32[8,256]{1,0:T(8,128)S(1)} all-reduce(f32[8,256]{1,0:T(8,128)S(1)} %convolution_select_fusion.11), channel_id=1, replica_groups=mesh['dp'=32,'crow'=4,'ccol'=4] {'crow','ccol'}, use_global_device_ids=true, to_apply=%region_34.35 | all-reduce | flops 2048 | bytes 16384 | tf_op jit(solution)/shard_map/psum | solution.py:102
  780.8 39.6 %psum.189 = f32[8,256]{1,0:T(8,128)S(1)} all-reduce(f32[8,256]{1,0:T(8,128)S(1)} %convolution_select_fusion.10), channel_id=1, replica_groups=mesh['dp'=32,'crow'=4,'ccol'=4] {'crow','ccol'}, use_global_device_ids=true, to_apply=%region_35.36 | all-reduce | flops 2048 | bytes 16384 | tf_op jit(solution)/shard_map/psum | solution.py:102
  822.0 36.0 %psum.190 = f32[8,256]{1,0:T(8,128)S(1)} all-reduce(f32[8,256]{1,0:T(8,128)S(1)} %convolution_select_fusion.9), channel_id=1, replica_groups=mesh['dp'=32,'crow'=4,'ccol'=4] {'crow','ccol'}, use_global_device_ids=true, to_apply=%region_36.37 | all-reduce | flops 2048 | bytes 16384 | tf_op jit(solution)/shard_map/psum | solution.py:102
  859.6 38.0 %psum.191 = f32[8,256]{1,0:T(8,128)S(1)} all-reduce(f32[8,256]{1,0:T(8,128)S(1)} %convolution_select_fusion.8), channel_id=1, replica_groups=mesh['dp'=32,'crow'=4,'ccol'=4] {'crow','ccol'}, use_global_device_ids=true, to_apply=%region_37.38 | all-reduce | flops 2048 | bytes 16384 | tf_op jit(solution)/shard_map/psum | solution.py:102
  899.3 36.1 %psum.192 = f32[8,256]{1,0:T(8,128)S(1)} all-reduce(f32[8,256]{1,0:T(8,128)S(1)} %convolution_select_fusion.7), channel_id=1, replica_groups=mesh['dp'=32,'crow'=4,'ccol'=4] {'crow','ccol'}, use_global_device_ids=true, to_apply=%region_38.39 | all-reduce | flops 2048 | bytes 16384 | tf_op jit(solution)/shard_map/psum | solution.py:102
  937.0 38.0 %psum.193 = f32[8,256]{1,0:T(8,128)S(1)} all-reduce(f32[8,256]{1,0:T(8,128)S(1)} %convolution_select_fusion.6), channel_id=1, replica_groups=mesh['dp'=32,'crow'=4,'ccol'=4] {'crow','ccol'}, use_global_device_ids=true, to_apply=%region_39.40 | all-reduce | flops 2048 | bytes 16384 | tf_op jit(solution)/shard_map/psum | solution.py:102
  976.5 36.1 %psum.194 = f32[8,256]{1,0:T(8,128)S(1)} all-reduce(f32[8,256]{1,0:T(8,128)S(1)} %convolution_select_fusion.5), channel_id=1, replica_groups=mesh['dp'=32,'crow'=4,'ccol'=4] {'crow','ccol'}, use_global_device_ids=true, to_apply=%region_40.41 | all-reduce | flops 2048 | bytes 16384 | tf_op jit(solution)/shard_map/psum | solution.py:102
  1014.2 37.9 %psum.195 = f32[8,256]{1,0:T(8,128)S(1)} all-reduce(f32[8,256]{1,0:T(8,128)S(1)} %convolution_select_fusion.4), channel_id=1, replica_groups=mesh['dp'=32,'crow'=4,'ccol'=4] {'crow','ccol'}, use_global_device_ids=true, to_apply=%region_41.42 | all-reduce | flops 2048 | bytes 16384 | tf_op jit(solution)/shard_map/psum | solution.py:102
  1053.8 36.2 %psum.196 = f32[8,256]{1,0:T(8,128)S(1)} all-reduce(f32[8,256]{1,0:T(8,128)S(1)} %convolution_select_fusion.3), channel_id=1, replica_groups=mesh['dp'=32,'crow'=4,'ccol'=4] {'crow','ccol'}, use_global_device_ids=true, to_apply=%region_42.43 | all-reduce | flops 2048 | bytes 16384 | tf_op jit(solution)/shard_map/psum | solution.py:102
  1091.7 37.8 %psum.197 = f32[8,256]{1,0:T(8,128)S(1)} all-reduce(f32[8,256]{1,0:T(8,128)S(1)} %convolution_select_fusion.2), channel_id=1, replica_groups=mesh['dp'=32,'crow'=4,'ccol'=4] {'crow','ccol'}, use_global_device_ids=true, to_apply=%region_43.44 | all-reduce | flops 2048 | bytes 16384 | tf_op jit(solution)/shard_map/psum | solution.py:102
  1131.1 36.2 %psum.198 = f32[8,256]{1,0:T(8,128)S(1)} all-reduce(f32[8,256]{1,0:T(8,128)S(1)} %convolution_select_fusion.1), channel_id=1, replica_groups=mesh['dp'=32,'crow'=4,'ccol'=4] {'crow','ccol'}, use_global_device_ids=true, to_apply=%region_44.45 | all-reduce | flops 2048 | bytes 16384 | tf_op jit(solution)/shard_map/psum | solution.py:102
  1169.0 37.8 %psum.199 = f32[8,256]{1,0:T(8,128)S(1)} all-reduce(f32[8,256]{1,0:T(8,128)S(1)} %convolution_select_fusion), channel_id=1, replica_groups=mesh['dp'=32,'crow'=4,'ccol'=4] {'crow','ccol'}, use_global_device_ids=true, to_apply=%region_45.46 | all-reduce | flops 2048 | bytes 16384 | tf_op jit(solution)/shard_map/psum | solution.py:102
  (121 shorter events, 75.1 us)
Async XLA Ops:
  7.2 91.3 %copy-start = (f32[768,768]{1,0:T(8,128)S(1)}, f32[768,768]{1,0:T(8,128)}, u32[]{:S(2)}) copy-start(f32[768,768]{1,0:T(8,128)} %param.63) | copy-start | bytes 7077892
  7.2 129.8 %copy-start.1 = (f32[3,256,256]{2,1,0:T(8,128)S(1)}, f32[3,256,256]{2,1,0:T(8,128)}, u32[]{:S(2)}) copy-start(f32[3,256,256]{2,1,0:T(8,128)} %param.64) | copy-start | bytes 2359300
  7.2 167.6 %copy-start.3 = (f32[8,3072]{1,0:T(8,128)S(1)}, f32[8,3072]{1,0:T(8,128)}, u32[]{:S(2)}) copy-start(f32[8,3072]{1,0:T(8,128)} %param.67) | copy-start | bytes 294916
  7.2 556.7 %all-reduce.4.cloned.1.call-start = ((), (), s32[]{:S(2)}) async-start(), calls=%async_computation | async-start | bytes 131072 | tf_op jit(solution)/shard_map/psum | solution.py:77
  328.7 165.1 %copy-start.7 = (f32[16,2048]{1,0:T(8,128)S(1)}, f32[16,2048]{1,0:T(8,128)}, u32[]{:S(2)}) copy-start(f32[16,2048]{1,0:T(8,128)} %param.60) | copy-start | bytes 393220
  329.2 166.4 %copy-start.2 = (f32[16,768]{1,0:T(8,128)S(1)}, f32[16,768]{1,0:T(8,128)}, u32[]{:S(2)}) copy-start(f32[16,768]{1,0:T(8,128)} %param.61) | copy-start | bytes 147460
  329.2 166.4 %copy-start.4 = (f32[16]{0:T(128)S(1)}, f32[16]{0:T(128)}, u32[]{:S(2)}) copy-start(f32[16]{0:T(128)} %param.62) | copy-start | bytes 196
  507.6 219.6 %all-gather.3.cloned.1.call-start = ((), (), s32[]{:S(2)}) async-start(), calls=%async_computation.1 | async-start | bytes 3170304 | tf_op jit(solution)/shard_map/all_gather | solution.py:86
  1052.8 154.7 %copy-start.5 = (f32[8,3072]{1,0:T(8,128)S(1)}, f32[8,3072]{1,0:T(8,128)}, u32[]{:S(2)}) copy-start(f32[8,3072]{1,0:T(8,128)} %param.66) | copy-start | bytes 294916
  1207.8 2.2 copy-start.6
Sparse Core Ops, SparseCore 0:
  507.7 56.1 all-reduce.3
  584.4 142.7 all-gather.2
